TPU v7x, 32 devices: a whole 2x2x4 slice. The times are simulated.
32 devices in a mesh: ang: 8 (over y, x, core), rad: 4 (over z).
Axes of the slice: x: 2, y: 2, z: 4, core: 2. Of those that a mesh axis runs over, the one named last changes fastest.
Arguments:
- coarse: float32 [1, 8, 32, 512], P(None, 'ang', None, 'rad'), may hold values from -6 to 6
- excite: float32 [1, 16, 64, 1024], P(None, 'ang', None, 'rad'), may hold values from -6 to 6
- kernels: float32 [27, 8, 512], replicated, may hold values from -0.875 to 0.875
- mixing: float32 [8, 8, 512], replicated, may hold values from -1.5 to 1.5
- star_bin: int32 [16, 64, 16], P('ang'), may hold values from 0 to 1023
- star_count: int32 [16, 64], P('ang'), may hold values from 1 to 16
- star_obs: float32 [16, 64, 16], P('ang'), may hold values from 0 to 3
- star_isig: float32 [16, 64, 16], P('ang'), may hold values from 1 to 10
Outputs:
- grad_excite: float32 [1, 16, 64, 1024], P(None, 'ang', None, 'rad')
- grad_coarse: float32 [1, 8, 32, 512], P(None, 'ang', None, 'rad')
All inputs are finite; a program needn't handle non-finite values.
Results may differ from a plain program's by a relative error of at most 0.0003.
Values sent between devices are 32-bit elements; how exact they have to be, the bound alone decides.
A program may use at most 64 MiB of HBM per device.

v0:
```python
import jax
import jax.numpy as jnp
from jax import lax
from jax.sharding import PartitionSpec as P


def extended(block, sides, width):
    for axis, dim in sides:
        count = lax.axis_size(axis)
        forward = [(i, i + 1) for i in range(count - 1)]
        backward = [(target, source) for source, target in forward]
        low = lax.ppermute(
            lax.slice_in_dim(block, block.shape[dim] - width, None, axis=dim), axis, forward
        )
        high = lax.ppermute(lax.slice_in_dim(block, 0, width, axis=dim), axis, backward)
        block = jnp.concatenate([low, block, high], axis=dim)
    return block


def to_blocks(field):
    samples, na, nb, nr = field.shape
    return (
        field.reshape(samples, na // 2, 2, nb // 2, 2, nr // 2, 2)
        .transpose(2, 4, 6, 0, 1, 3, 5)
        .reshape(8, samples, na // 2, nb // 2, nr // 2)
    )


def from_blocks(blocks):
    _, samples, na, nb, nr = blocks.shape
    return (
        blocks.reshape(2, 2, 2, samples, na, nb, nr)
        .transpose(3, 4, 0, 5, 1, 6, 2)
        .reshape(samples, 2 * na, 2 * nb, 2 * nr)
    )


def per_device(coarse, excite, kernels, mixing, star_bin, star_count, star_obs, star_isig):
    samples, rows_c, cols_c, depth_c = coarse.shape
    rows_f, cols_f, depth_f = (2 * rows_c, 2 * cols_c, 2 * depth_c)
    rad_index = lax.axis_index("rad")
    rad_count = lax.axis_size("rad")
    step_len = 1.0 / (depth_f * rad_count)
    kernel_pad = jnp.pad(kernels, ((0, 0), (0, 0), (1, 1)), mode="edge")
    kernel_wide = lax.dynamic_slice_in_dim(kernel_pad, rad_index * depth_c, depth_c + 2, 2)
    kernel_here = kernel_wide[:, :, 1:-1]
    mixing_here = lax.dynamic_slice_in_dim(mixing, rad_index * depth_c, depth_c, 2)
    framed = extended(coarse, (("ang", 1), ("rad", 3)), 1)
    framed = jnp.pad(framed, ((0, 0), (0, 0), (1, 1), (0, 0)))
    fine = jnp.zeros((8, samples, rows_c, cols_c, depth_c), jnp.float32)
    for offset in range(27):
        step_a, step_b, step_r = (offset // 9, offset // 3 % 3, offset % 3)
        window = framed[
            :, step_a : step_a + rows_c, step_b : step_b + cols_c, step_r : step_r + depth_c
        ]
        fine = fine + kernel_here[offset][:, None, None, None, :] * window[None]
    excite_blocks = to_blocks(excite)
    fine = fine + jnp.einsum(
        "qpr,psabr->qsabr", mixing_here, excite_blocks, precision=lax.Precision.HIGHEST
    )
    dens = jnp.exp(from_blocks(fine))
    ladder = jnp.arange(depth_f)
    upper = (ladder[:, None] <= ladder[None, :]).astype(jnp.float32)
    cumul = jnp.dot(dens.reshape(-1, depth_f), upper, precision=lax.Precision.HIGHEST).reshape(
        dens.shape
    )
    depth_sums = cumul[..., -1]
    every = lax.all_gather(depth_sums[None], "rad", axis=0, tiled=True)
    below = jnp.arange(every.shape[0]) < rad_index
    nearer = jnp.sum(jnp.where(below[:, None, None, None], every, 0.0), axis=0)
    extinction = step_len * (nearer[..., None] + cumul)
    local_bin = star_bin - rad_index * depth_f
    live = jnp.arange(star_bin.shape[2])[None, None, :] < star_count[:, :, None]
    inside = live & (local_bin >= 0) & (local_bin < depth_f)
    clipped = jnp.clip(local_bin, 0, depth_f - 1)
    pred = jnp.take_along_axis(extinction, clipped[None], axis=3)
    res = jnp.where(inside[None], (pred - star_obs[None]) * star_isig[None], 0.0)
    terms = res * star_isig[None]
    onehot = ((clipped[..., None] == ladder) & inside[..., None]).astype(jnp.float32)
    hits = jnp.einsum("sabm,abmr->sabr", terms, onehot, precision=lax.Precision.HIGHEST)
    suffix = jnp.dot(hits.reshape(-1, depth_f), upper.T, precision=lax.Precision.HIGHEST).reshape(
        hits.shape
    )
    star_sums = suffix[..., 0]
    every_star = lax.all_gather(star_sums[None], "rad", axis=0, tiled=True)
    above = jnp.arange(every_star.shape[0]) > rad_index
    farther = jnp.sum(jnp.where(above[:, None, None, None], every_star, 0.0), axis=0)
    grad_fine = to_blocks(dens * step_len * (farther[..., None] + suffix))
    grad_excite = from_blocks(
        jnp.einsum("qpr,qsabr->psabr", mixing_here, grad_fine, precision=lax.Precision.HIGHEST)
        + excite_blocks
    )
    framed_grad = extended(grad_fine, (("ang", 2), ("rad", 4)), 1)
    framed_grad = jnp.pad(framed_grad, ((0, 0), (0, 0), (0, 0), (1, 1), (0, 0)))
    grad_coarse = jnp.zeros((samples, rows_c, cols_c, depth_c), jnp.float32)
    for offset in range(27):
        step_a, step_b, step_r = (offset // 9, offset // 3 % 3, offset % 3)
        piece = framed_grad[
            :,
            :,
            2 - step_a : 2 - step_a + rows_c,
            2 - step_b : 2 - step_b + cols_c,
            2 - step_r : 2 - step_r + depth_c,
        ]
        weights = kernel_wide[offset][:, 2 - step_r : 2 - step_r + depth_c]
        grad_coarse = grad_coarse + jnp.sum(weights[:, None, None, None, :] * piece, axis=0)
    return (grad_excite, grad_coarse)


def solution(mesh):
    in_specs = (
        P(None, "ang", None, "rad"),
        P(None, "ang", None, "rad"),
        P(),
        P(),
        P("ang", None, None),
        P("ang", None),
        P("ang", None, None),
        P("ang", None, None),
    )
    out_specs = (P(None, "ang", None, "rad"), P(None, "ang", None, "rad"))
    return jax.shard_map(
        per_device, mesh=mesh, in_specs=in_specs, out_specs=out_specs, check_vma=False
    )
```

profile of v0, /device:TPU:1, one launch (start us, length us, event | category | flops | bytes accessed | tf_op | source)
XLA Modules:
  0.0 213.7 jit_solution(2497887783961460877)
XLA Ops:
  0.6 2.1 collective-permute-start.1
  2.8 4.5 %collective-permute-start = (f32[1,1,32,128]{3,2,1,0:T(8,128)}, f32[1,1,32,128]{3,2,1,0:T(8,128)S(1)}, u32[]{:S(2)}, u32[]{:S(2)}) collective-permute-start(f32[1,1,32,128]{3,2,1,0:T(8,128)} %param.8), channel_id=1, source_target_pairs={{0,4},{4,8},{8,12},{12,16},{16,20},{20,24},{24,28},{1,5},{5,9},{9,... | collective-permute-start | bytes 49160 | tf_op jit(solution)/shard_map/ppermute | solution.py:12
  11.2 10.5 %reshape.843 = f32[1,1,2,32,2,128,2]{6,5,4,3,2,1,0:T(8,128)} reshape(f32[1,2,64,256]{3,2,1,0:T(8,128)} %param.9) | data formatting | bytes 262144 | tf_op jit(solution)/shard_map/reshape | solution.py:23
  21.7 5.3 %copy.292 = f32[2,2,2,1,1,32,128]{6,5,2,1,0,4,3:T(8,128)S(1)} copy(f32[2,2,2,1,1,32,128]{2,6,1,5,0,4,3:T(8,128)} %bitcast.271) | data formatting | bytes 262144 | tf_op jit(solution)/shard_map/transpose | solution.py:24
  27.0 8.4 %copy.305 = f32[2,2,2,1,1,32,128]{5,2,1,0,6,4,3:T(2,128)S(1)} copy(f32[2,2,2,1,1,32,128]{2,6,1,5,0,4,3:T(8,128)} %bitcast.272) | data formatting | bytes 262144 | tf_op jit(solution)/shard_map/transpose | solution.py:24
  55.7 3.2 %collective-permute-start.2 = (f32[1,3,32,1]{3,2,1,0:T(8,128)S(1)}, f32[1,3,32,1]{3,2,1,0:T(8,128)S(1)}, u32[]{:S(2)}, u32[]{:S(2)}) collective-permute-start(f32[1,3,32,1]{3,2,1,0:T(8,128)S(1)} %get-tuple-element.119), channel_id=1, source_target_pairs={{0,1},{1,2},{2,3},{4,5},{5,6},{6,7},{8,9},{9,10},{10,11},{12,13},{... | collective-permute-start | bytes 1160 | tf_op jit(solution)/shard_map/ppermute | solution.py:12
  59.0 1.3 collective-permute-start.3
  61.5 3.0 %collective-permute-done.3 = f32[1,3,32,1]{3,2,1,0:T(8,128)S(1)} collective-permute-done((f32[1,3,32,1]{3,2,1,0:T(8,128)S(1)}, f32[1,3,32,1]{3,2,1,0:T(8,128)S(1)}, u32[]{:S(2)}, u32[]{:S(2)}) %collective-permute-start.3) | collective-permute-done | bytes 416 | tf_op jit(solution)/shard_map/ppermute | solution.py:15
  80.2 7.6 %broadcast_multiply_fusion = (f32[8,1,1,32,128]{3,0,4,2,1:T(8,128)S(1)}, f32[8,1,1,32,128]{3,0,4,2,1:T(8,128)S(1)}) fusion(f32[8,8,128]{1,0,2:T(8,128)S(1)} %copy.312, f32[8,32,128]{1,0,2:T(8,128)} %copy.293, f32[32,128]{0,1:T(8,128)} %copy.290, f32[8,128]{0,1:T(8,128)} %copy.289, f32[32,128]{0,1:T(8,128)} %copy.288, f32[8,128]{0,1:T(8,128)} %copy.287, ...), kind=kOutput, calls=%fused_computation.28 | convolution fusion | flops 4947968 | bytes 978944 | tf_op jit(solution)/shard_map/qpr,psabr->qsabr/dot_general | solution.py:58
  87.8 8.0 %copy.296 = f32[2,2,2,1,1,32,128]{2,6,1,5,0,4,3:T(8,128)} copy(f32[2,2,2,1,1,32,128]{5,2,1,0,6,4,3:T(2,128)S(1)} %bitcast.289) | data formatting | bytes 262144 | tf_op jit(solution)/shard_map/exp | solution.py:61
  95.8 6.9 %exp.22 = f32[128,256]{1,0:T(8,128)S(1)} reshape(f32[1,1,2,32,2,128,2]{6,5,4,3,2,1,0:T(8,128)} %bitcast.273) | data formatting | bytes 262144 | tf_op jit(solution)/shard_map/exp | solution.py:61
  103.1 7.3 %all-gather = f32[4,2,64,1]{2,1,3,0:T(2,128)S(1)} all-gather(f32[1,2,64,1]{2,1,3,0:T(2,128)S(1)} %copy.297), channel_id=2, replica_groups=mesh['ang'=8,'rad'=4] {'rad'}, dimensions={0}, use_global_device_ids=true | all-gather | bytes 2560 | tf_op jit(solution)/shard_map/all_gather | solution.py:68
  110.6 20.6 %gather_fusion = f32[2048]{0:T(1024)S(1)} fusion(f32[2,64,256]{2,1,0:T(8,128)S(1)} %multiply_bitcast_fusion, s32[2048]{0:T(1024)S(1)} %reshape.860), kind=kCustom, calls=%fused_computation | custom fusion | bytes 40960 | tf_op jit(solution)/shard_map/jit(take_along_axis)/gather | solution.py:76
  133.0 9.7 %reshape.848 = f32[1,1,2,32,2,128,2]{6,5,4,3,2,1,0:T(8,128)} reshape(f32[128,256]{1,0:T(8,128)S(1)} %fusion.10) | data formatting | bytes 262144 | tf_op jit(solution)/shard_map/reshape | solution.py:81
  142.8 6.2 %all-gather.1 = f32[4,2,64,1]{2,1,3,0:T(2,128)S(1)} all-gather(f32[1,2,64,1]{2,1,3,0:T(2,128)S(1)} %copy.313), channel_id=3, replica_groups=mesh['ang'=8,'rad'=4] {'rad'}, dimensions={0}, use_global_device_ids=true | all-gather | bytes 2560 | tf_op jit(solution)/shard_map/all_gather | solution.py:85
  149.2 8.0 %copy.294 = f32[2,2,2,1,1,32,128]{2,6,1,5,0,4,3:T(8,128)} copy(f32[2,2,2,1,1,32,128]{5,2,1,0,6,4,3:T(2,128)S(1)} %bitcast.288) | data formatting | bytes 262144 | tf_op jit(solution)/shard_map/mul | solution.py:88
  157.2 10.0 %multiply_reduce_fusion = (f32[32,128]{1,0:T(8,128)S(1)}, f32[2,2,2,1,1,32,128]{2,6,1,5,0,4,3:T(8,128)}) fusion(f32[2,2,2,128]{2,3,1,0:T(8,128)S(1)} %copy.308, f32[1,1,2,32,2,128,2]{6,5,4,3,2,1,0:T(8,128)} %reshape.848, f32[2,32,2]{2,1,0:T(8,128)S(1)} %add.668, f32[2,2,2,1,1,32,128]{2,6,1,5,0,4,3:T(8,128)} %copy.294), kind=kLoop, calls=%fused_computation.3 | loop fusion | flops 126976 | bytes 414208 | tf_op jit(solution)/shard_map/reduce_sum | solution.py:106
  167.3 5.3 %copy.302 = f32[2,2,2,1,1,32,128]{6,5,2,1,0,4,3:T(8,128)S(1)} copy(f32[2,2,2,1,1,32,128]{2,6,1,5,0,4,3:T(8,128)} %get-tuple-element.29) | data formatting | bytes 262144 | tf_op jit(solution)/shard_map/transpose | solution.py:24
  172.6 6.5 %collective-permute-start.5 = (f32[8,1,1,32,128]{4,3,0,2,1:T(8,128)S(1)}, f32[8,1,1,32,128]{4,3,0,2,1:T(8,128)S(1)}, u32[]{:S(2)}, u32[]{:S(2)}) collective-permute-start(f32[8,1,1,32,128]{4,3,0,2,1:T(8,128)S(1)} %bitcast.275), channel_id=1, source_target_pairs={{4,0},{8,4},{12,8},{16,12},{20,16},{24,20},{28,24},{5,1},{9,5},{13... | collective-permute-start | bytes 393224 | tf_op jit(solution)/shard_map/ppermute | solution.py:15
  179.1 2.6 %collective-permute-start.4 = (f32[8,1,1,32,128]{4,3,0,2,1:T(8,128)S(1)}, f32[8,1,1,32,128]{4,3,0,2,1:T(8,128)S(1)}, u32[]{:S(2)}, u32[]{:S(2)}) collective-permute-start(f32[8,1,1,32,128]{4,3,0,2,1:T(8,128)S(1)} %bitcast.276), channel_id=1, source_target_pairs={{0,4},{4,8},{8,12},{12,16},{16,20},{20,24},{24,28},{1,5},{5,9},{9,... | collective-permute-start | bytes 393224 | tf_op jit(solution)/shard_map/ppermute | solution.py:12
  190.3 3.1 %collective-permute-start.6 = (f32[8,1,3,32,1]{4,3,0,2,1:T(8,128)}, f32[8,1,3,32,1]{4,3,0,2,1:T(8,128)S(1)}, u32[]{:S(2)}, u32[]{:S(2)}) collective-permute-start(f32[8,1,3,32,1]{4,3,0,2,1:T(8,128)} %get-tuple-element.36), channel_id=1, source_target_pairs={{0,1},{1,2},{2,3},{4,5},{5,6},{6,7},{8,9},{9,10},{10,11},{12,13},{... | collective-permute-start | bytes 9224 | tf_op jit(solution)/shard_map/ppermute | solution.py:12
  193.4 1.3 collective-permute-start.7
  196.0 8.0 %copy.306 = f32[2,2,2,1,1,32,128]{2,6,1,5,0,4,3:T(8,128)} copy(f32[2,2,2,1,1,32,128]{5,2,1,0,6,4,3:T(2,128)S(1)} %bitcast.283) | data formatting | bytes 262144 | tf_op jit(solution)/shard_map/reshape | solution.py:32
  204.0 7.5 %reshape.852 = f32[1,2,64,256]{3,2,1,0:T(8,128)} reshape(f32[1,1,2,32,2,128,2]{6,5,4,3,2,1,0:T(8,128)} %bitcast.274) | data formatting | bytes 262144 | tf_op jit(solution)/shard_map/reshape | solution.py:34
  (196 shorter events, 55.6 us)
Async XLA Ops:
  0.6 55.0 %collective-permute-start.1 = (f32[1,1,32,128]{3,2,1,0:T(8,128)}, f32[1,1,32,128]{3,2,1,0:T(8,128)S(1)}, u32[]{:S(2)}, u32[]{:S(2)}) collective-permute-start(f32[1,1,32,128]{3,2,1,0:T(8,128)} %param.8), channel_id=1, source_target_pairs={{4,0},{8,4},{12,8},{16,12},{20,16},{24,20},{28,24},{5,1},{9,5},{13... | collective-permute-start | bytes 49160 | tf_op jit(solution)/shard_map/ppermute | solution.py:15
  2.8 52.8 %collective-permute-start = (f32[1,1,32,128]{3,2,1,0:T(8,128)}, f32[1,1,32,128]{3,2,1,0:T(8,128)S(1)}, u32[]{:S(2)}, u32[]{:S(2)}) collective-permute-start(f32[1,1,32,128]{3,2,1,0:T(8,128)} %param.8), channel_id=1, source_target_pairs={{0,4},{4,8},{8,12},{12,16},{16,20},{20,24},{24,28},{1,5},{5,9},{9,... | collective-permute-start | bytes 49160 | tf_op jit(solution)/shard_map/ppermute | solution.py:12
  55.7 5.7 %collective-permute-start.2 = (f32[1,3,32,1]{3,2,1,0:T(8,128)S(1)}, f32[1,3,32,1]{3,2,1,0:T(8,128)S(1)}, u32[]{:S(2)}, u32[]{:S(2)}) collective-permute-start(f32[1,3,32,1]{3,2,1,0:T(8,128)S(1)} %get-tuple-element.119), channel_id=1, source_target_pairs={{0,1},{1,2},{2,3},{4,5},{5,6},{6,7},{8,9},{9,10},{10,11},{12,13},{... | collective-permute-start | bytes 1160 | tf_op jit(solution)/shard_map/ppermute | solution.py:12
  59.0 5.5 %collective-permute-start.3 = (f32[1,3,32,1]{3,2,1,0:T(8,128)S(1)}, f32[1,3,32,1]{3,2,1,0:T(8,128)S(1)}, u32[]{:S(2)}, u32[]{:S(2)}) collective-permute-start(f32[1,3,32,1]{3,2,1,0:T(8,128)S(1)} %get-tuple-element.120), channel_id=1, source_target_pairs={{1,0},{2,1},{3,2},{5,4},{6,5},{7,6},{9,8},{10,9},{11,10},{13,12},{... | collective-permute-start | bytes 1160 | tf_op jit(solution)/shard_map/ppermute | solution.py:15
  110.6 20.7 %copy-start.29 = (s32[2,64]{1,0:T(2,128)S(1)}, s32[2,64]{1,0:T(2,128)}, u32[]{:S(2)}) copy-start(s32[2,64]{1,0:T(2,128)} %param.13) | copy-start | bytes 1540
  167.1 19.7 %copy-start.16 = (f32[8,130]{1,0:T(8,128)S(1)}, f32[8,130]{1,0:T(8,128)}, u32[]{:S(2)}) copy-start(f32[8,130]{1,0:T(8,128)} %get-tuple-element.38) | copy-start | bytes 12484
  167.1 20.4 %copy-start.15 = (f32[8,130]{1,0:T(8,128)S(1)}, f32[8,130]{1,0:T(8,128)}, u32[]{:S(2)}) copy-start(f32[8,130]{1,0:T(8,128)} %get-tuple-element.39) | copy-start | bytes 12484
  167.1 21.0 %copy-start.14 = (f32[8,130]{1,0:T(8,128)S(1)}, f32[8,130]{1,0:T(8,128)}, u32[]{:S(2)}) copy-start(f32[8,130]{1,0:T(8,128)} %get-tuple-element.40) | copy-start | bytes 12484
  167.1 21.1 %copy-start.13 = (f32[8,130]{1,0:T(8,128)S(1)}, f32[8,130]{1,0:T(8,128)}, u32[]{:S(2)}) copy-start(f32[8,130]{1,0:T(8,128)} %get-tuple-element.41) | copy-start | bytes 12484
  167.2 21.1 %copy-start.12 = (f32[8,130]{1,0:T(8,128)S(1)}, f32[8,130]{1,0:T(8,128)}, u32[]{:S(2)}) copy-start(f32[8,130]{1,0:T(8,128)} %get-tuple-element.42) | copy-start | bytes 12484
  167.2 21.1 %copy-start.11 = (f32[8,130]{1,0:T(8,128)S(1)}, f32[8,130]{1,0:T(8,128)}, u32[]{:S(2)}) copy-start(f32[8,130]{1,0:T(8,128)} %get-tuple-element.43) | copy-start | bytes 12484
  167.2 21.2 %copy-start.10 = (f32[8,130]{1,0:T(8,128)S(1)}, f32[8,130]{1,0:T(8,128)}, u32[]{:S(2)}) copy-start(f32[8,130]{1,0:T(8,128)} %get-tuple-element.44) | copy-start | bytes 12484
  167.2 21.2 %copy-start.9 = (f32[8,130]{1,0:T(8,128)S(1)}, f32[8,130]{1,0:T(8,128)}, u32[]{:S(2)}) copy-start(f32[8,130]{1,0:T(8,128)} %get-tuple-element.45) | copy-start | bytes 12484
  167.2 21.3 %copy-start.8 = (f32[8,130]{1,0:T(8,128)S(1)}, f32[8,130]{1,0:T(8,128)}, u32[]{:S(2)}) copy-start(f32[8,130]{1,0:T(8,128)} %get-tuple-element.46) | copy-start | bytes 12484
  167.2 21.3 %copy-start.7 = (f32[8,130]{1,0:T(8,128)S(1)}, f32[8,130]{1,0:T(8,128)}, u32[]{:S(2)}) copy-start(f32[8,130]{1,0:T(8,128)} %get-tuple-element.47) | copy-start | bytes 12484
  167.2 21.3 %copy-start.6 = (f32[8,130]{1,0:T(8,128)S(1)}, f32[8,130]{1,0:T(8,128)}, u32[]{:S(2)}) copy-start(f32[8,130]{1,0:T(8,128)} %get-tuple-element.48) | copy-start | bytes 12484
  167.2 21.4 %copy-start.5 = (f32[8,130]{1,0:T(8,128)S(1)}, f32[8,130]{1,0:T(8,128)}, u32[]{:S(2)}) copy-start(f32[8,130]{1,0:T(8,128)} %get-tuple-element.49) | copy-start | bytes 12484
  167.2 21.5 %copy-start.4 = (f32[8,130]{1,0:T(8,128)S(1)}, f32[8,130]{1,0:T(8,128)}, u32[]{:S(2)}) copy-start(f32[8,130]{1,0:T(8,128)} %get-tuple-element.50) | copy-start | bytes 12484
  167.2 21.5 %copy-start.3 = (f32[8,130]{1,0:T(8,128)S(1)}, f32[8,130]{1,0:T(8,128)}, u32[]{:S(2)}) copy-start(f32[8,130]{1,0:T(8,128)} %get-tuple-element.52) | copy-start | bytes 12484
  167.2 21.5 %copy-start.2 = (f32[8,130]{1,0:T(8,128)S(1)}, f32[8,130]{1,0:T(8,128)}, u32[]{:S(2)}) copy-start(f32[8,130]{1,0:T(8,128)} %get-tuple-element.53) | copy-start | bytes 12484
  172.6 16.6 %collective-permute-start.5 = (f32[8,1,1,32,128]{4,3,0,2,1:T(8,128)S(1)}, f32[8,1,1,32,128]{4,3,0,2,1:T(8,128)S(1)}, u32[]{:S(2)}, u32[]{:S(2)}) collective-permute-start(f32[8,1,1,32,128]{4,3,0,2,1:T(8,128)S(1)} %bitcast.275), channel_id=1, source_target_pairs={{4,0},{8,4},{12,8},{16,12},{20,16},{24,20},{28,24},{5,1},{9,5},{13... | collective-permute-start | bytes 393224 | tf_op jit(solution)/shard_map/ppermute | solution.py:15
  179.1 10.1 %collective-permute-start.4 = (f32[8,1,1,32,128]{4,3,0,2,1:T(8,128)S(1)}, f32[8,1,1,32,128]{4,3,0,2,1:T(8,128)S(1)}, u32[]{:S(2)}, u32[]{:S(2)}) collective-permute-start(f32[8,1,1,32,128]{4,3,0,2,1:T(8,128)S(1)} %bitcast.276), channel_id=1, source_target_pairs={{0,4},{4,8},{8,12},{12,16},{16,20},{20,24},{24,28},{1,5},{5,9},{9,... | collective-permute-start | bytes 393224 | tf_op jit(solution)/shard_map/ppermute | solution.py:12
  190.3 21.2 %collective-permute-start.6 = (f32[8,1,3,32,1]{4,3,0,2,1:T(8,128)}, f32[8,1,3,32,1]{4,3,0,2,1:T(8,128)S(1)}, u32[]{:S(2)}, u32[]{:S(2)}) collective-permute-start(f32[8,1,3,32,1]{4,3,0,2,1:T(8,128)} %get-tuple-element.36), channel_id=1, source_target_pairs={{0,1},{1,2},{2,3},{4,5},{5,6},{6,7},{8,9},{9,10},{10,11},{12,13},{... | collective-permute-start | bytes 9224 | tf_op jit(solution)/shard_map/ppermute | solution.py:12
  193.4 18.0 %collective-permute-start.7 = (f32[8,1,3,32,1]{4,3,0,2,1:T(8,128)}, f32[8,1,3,32,1]{4,3,0,2,1:T(8,128)S(1)}, u32[]{:S(2)}, u32[]{:S(2)}) collective-permute-start(f32[8,1,3,32,1]{4,3,0,2,1:T(8,128)} %get-tuple-element.37), channel_id=1, source_target_pairs={{1,0},{2,1},{3,2},{5,4},{6,5},{7,6},{9,8},{10,9},{11,10},{13,12},{... | collective-permute-start | bytes 9224 | tf_op jit(solution)/shard_map/ppermute | solution.py:15
  (14 other events, 190.4 us)
where the time goes:
time: 215 us; the launch traced here: 214 us
  local copies, waits for them, and re-layouts  147 us (68%)
  starting transfers between devices  24.6 us (11%)
  other arithmetic  13.9 us (6%)
  blocking collectives  13.4 us (6%)
  matrix products  10.6 us (5%)
  waiting for transfers between devices  3.03 us (1%)
    mul x57, local copies, waits for them, and re-layouts, per_device(): fine = fine + kernel_here[offset][:, None, None, None, :] * window[None]  35.3 us
    gather x3, local copies, waits for them, and re-layouts, per_device(): pred = jnp.take_along_axis(extinction, clipped[None], axis=3)  20.7 us
    transpose x3, local copies, waits for them, and re-layouts, to_blocks(): return field.reshape(samples, na // 2, 2, nb // 2, 2, nr // 2, 2).transpo...  19 us
    exp x2, local copies, waits for them, and re-layouts, per_device(): dens = jnp.exp(from_blocks(fine))  14.9 us
    ppermute x4, starting transfers between devices, extended(): lax.ppermute(lax.slice_in_dim(block, block.shape[dim] - width, None, axis...  13.4 us
    ppermute x4, starting transfers between devices, extended(): lax.ppermute(lax.slice_in_dim(block, 0, width, axis=dim), axis, backward)  11.2 us
    reduce_sum x5, other arithmetic, per_device(): jnp.sum(weights[:, None, None, None, :] * piece, axis=0)  11 us
    reshape x1, local copies, waits for them, and re-layouts, to_blocks(): field.reshape(samples, na // 2, 2, nb // 2, 2, nr // 2, 2)  10.5 us
  transfers between devices with their start and end apart: 8, of which 1 were waited for; matrix products, arithmetic and copies ran while one was open for 34% of the time, Pallas kernels for 0%

commit v1 on v0

v1 whole, which is shorter than its diff:
```python
import functools

import jax
import jax.numpy as jnp
from jax import lax
from jax.experimental import pallas as pl
from jax.experimental.pallas import tpu as pltpu
from jax.sharding import PartitionSpec as P

MESH = pl.DeviceIdType.MESH
AROUND = [(du, dz) for du in (-1, 0, 1) for dz in (-1, 0, 1) if (du, dz) != (0, 0)]
PAD = 8


def kernel(
    n_ang,
    n_rad,
    coarse_hbm,
    excite_hbm,
    weights_hbm,
    mixing_hbm,
    bin_hbm,
    count_hbm,
    obs_hbm,
    isig_hbm,
    grad_excite_hbm,
    grad_coarse_hbm,
    coarse,
    excite,
    weights,
    mixing,
    bins,
    count,
    obs,
    isig,
    edge_out,
    halo_rows,
    halo_edges,
    windows,
    blocks,
    dens,
    mine,
    parts,
    slopes,
    back_rows_out,
    back_edges_out,
    back_rows,
    back_edges,
    out_excite,
    out_coarse,
    load_sem,
    halo_send,
    halo_recv,
    part_send,
    part_recv,
    back_send,
    back_recv,
    store_sem,
):
    ang = lax.axis_index("ang")
    rad = lax.axis_index("rad")
    cols, depth = coarse.shape
    slots = mine.shape[0]
    half = depth // 2
    step_len = 1.0 / (2 * depth * n_rad)
    f32 = jnp.float32

    def exists(du, dz):
        there = None
        for shift, place, size in ((du, ang, n_ang), (dz, rad, n_rad)):
            if shift == 0:
                continue
            ok = place > 0 if shift < 0 else place < size - 1
            there = ok if there is None else jnp.logical_and(there, ok)
        return there

    def at(du, dz):
        return {"ang": ang + du, "rad": rad + dz}

    def peer(k):
        return {"ang": ang, "rad": lax.rem(rad + k, n_rad)}

    here = pl.ds(pl.multiple_of(rad * depth, depth), depth)
    pairs = [
        (coarse_hbm, coarse),
        (excite_hbm.at[:, :, pl.ds(0, depth)], excite.at[0]),
        (excite_hbm.at[:, :, pl.ds(depth, depth)], excite.at[1]),
        (mixing_hbm.at[:, :, here], mixing),
        (weights_hbm.at[:, :, here], weights),
        (bin_hbm, bins),
        (count_hbm, count),
        (obs_hbm, obs),
        (isig_hbm, isig),
    ]
    loads = [
        pltpu.make_async_copy(source, target, load_sem.at[n])
        for n, (source, target) in enumerate(pairs)
    ]
    for load in loads:
        load.start()

    barrier = pltpu.get_barrier_semaphore()
    beside = [(du, dz) for du, dz in AROUND if du != 0]
    for du, dz in beside:

        @pl.when(exists(du, dz))
        def _():
            pl.semaphore_signal(barrier, inc=1, device_id=at(du, dz), device_id_type=MESH)

    for k in range(1, n_rad):
        pl.semaphore_signal(barrier, inc=1, device_id=peer(k), device_id_type=MESH)

    rows_of = lambda du: 0 if du < 0 else 1
    halo_copies, back_copies = [], []
    for n, (du, dz) in enumerate(AROUND):
        if dz == 0:
            source, target = coarse, halo_rows.at[rows_of(-du)]
            back_source, back_target = back_rows_out.at[rows_of(du)], back_rows.at[rows_of(-du)]
        else:
            source, target = edge_out.at[rows_of(dz)], halo_edges.at[rows_of(-dz), 1 - du]
            back_source = back_edges_out.at[rows_of(dz), 1 + du]
            back_target = back_edges.at[rows_of(-dz), 1 - du]
        halo_copies.append(
            pltpu.make_async_remote_copy(
                src_ref=source, dst_ref=target, send_sem=halo_send.at[n],
                recv_sem=halo_recv.at[n], device_id=at(du, dz), device_id_type=MESH,
            )
        )
        back_copies.append(
            pltpu.make_async_remote_copy(
                src_ref=back_source, dst_ref=back_target, send_sem=back_send.at[n],
                recv_sem=back_recv.at[n], device_id=at(du, dz), device_id_type=MESH,
            )
        )

        @pl.when(jnp.logical_not(exists(-du, -dz)))
        def _():
            target[...] = jnp.zeros(target.shape, f32)
            back_target[...] = jnp.zeros(back_target.shape, f32)

    lane = lax.broadcasted_iota(jnp.int32, (cols, depth), 1)
    row = lax.broadcasted_iota(jnp.int32, (cols, depth), 0)
    diagonal = lane == row

    def pack(column):
        return jnp.sum(jnp.where(diagonal, column, 0.0), axis=0, keepdims=True)

    def unpack(packed):
        return jnp.sum(jnp.where(diagonal, packed, 0.0), axis=1, keepdims=True)

    loads[0].wait()
    middle = coarse[...]
    edge_out[0] = pack(middle[:, 0:1])
    edge_out[1] = pack(middle[:, depth - 1 : depth])

    sides = [jnp.where(place > 0, 1, 0) + jnp.where(place < size - 1, 1, 0)
             for place, size in ((ang, n_ang), (rad, n_rad))]
    pl.semaphore_wait(barrier, sides[0] * (sides[1] + 1) + n_rad - 1)
    for n, (du, dz) in enumerate(AROUND):
        pl.when(exists(du, dz))(halo_copies[n].start)

    for load in loads[1:]:
        load.wait()

    place = lax.broadcasted_iota(jnp.int32, (slots, depth), 1)
    slot = lax.broadcasted_iota(jnp.int32, (slots, depth), 0)
    group, member = place // cols, place % cols
    order = (group // 2) * (2 * cols) + 2 * member + group % 2

    def wide(ref):
        return jnp.concatenate([ref[0], ref[1]], axis=1)

    def picked(values, index):
        return jnp.take_along_axis(values, index, axis=1, mode="promise_in_bounds")

    counts = jnp.concatenate([count[0:1], count[1:2]], axis=1)
    inverse = picked(jnp.where(slot < counts, wide(isig), 0.0), order)
    live = inverse > 0.0
    observed = picked(wide(obs), order)
    local = picked(wide(bins), order) - rad * (2 * depth)

    evens = (2 * lane) % depth + lane // half
    odds = (2 * lane + 1) % depth - lane // half
    children = [None] * 8
    for i in range(2):
        for j in range(2):
            low = picked(excite[0, i, pl.ds(j, cols, stride=2), :], evens)
            high = picked(excite[1, i, pl.ds(j, cols, stride=2), :], odds)
            q = 4 * i + 2 * j
            children[q] = jnp.where(lane < half, low, high)
            children[q + 1] = pltpu.roll(jnp.where(lane < half, high, low), half, 1)
            blocks[q] = children[q]
            blocks[q + 1] = children[q + 1]
    fine = []
    for q in range(8):
        total = mixing[q, 0:1, :] * children[0]
        for p in range(1, 8):
            total = total + mixing[q, p : p + 1, :] * children[p]
        fine.append(total)

    blank = jnp.zeros((PAD, depth), f32)
    for u in range(3):
        for w in range(3):
            windows[u, w, 0:PAD] = blank
            windows[u, w, PAD + cols : 2 * PAD + cols] = blank
    for q in range(8):
        slopes[q, 0:PAD] = blank
        slopes[q, PAD + cols : 2 * PAD + cols] = blank

    def gather(u, base):
        near, far = unpack(halo_edges[0, u]), unpack(halo_edges[1, u])
        inner = pl.ds(PAD, cols)
        windows[u, 0, inner] = jnp.where(lane == 0, near, pltpu.roll(base, 1, 1))
        windows[u, 1, inner] = base
        windows[u, 2, inner] = jnp.where(lane == depth - 1, far, pltpu.roll(base, depth - 1, 1))

    def spread(u, ws, fine):
        for v in range(3):
            for w in ws:
                window = windows[u, w, PAD - 1 + v : PAD - 1 + v + cols, :]
                t = 9 * u + 3 * v + w
                fine = [
                    fine[q] + weights[t, q : q + 1, :] * window for q in range(8)
                ]
        return fine

    windows[1, 1, PAD : PAD + cols] = middle
    fine = spread(1, (1,), fine)
    for n, (du, dz) in enumerate(AROUND):
        pl.when(exists(-du, -dz))(halo_copies[n].wait_recv)
    gather(1, middle)
    gather(0, halo_rows[0])
    gather(2, halo_rows[1])
    fine = spread(1, (0, 2), fine)
    fine = spread(0, (0, 1, 2), fine)
    fine = spread(2, (0, 1, 2), fine)
    for q in range(8):
        dens[q] = jnp.exp(fine[q])

    pixels = 4 * cols
    ladder = 2 * lax.broadcasted_iota(jnp.int32, (depth, pixels), 0)
    first = jnp.concatenate([dens[q] for q in range(0, 8, 2)], axis=0).T
    second = jnp.concatenate([dens[q] for q in range(1, 8, 2)], axis=0).T
    for m in range(slots):
        limit = local[m : m + 1, :]
        mine[m : m + 1, :] = jnp.sum(
            jnp.where(ladder <= limit, first, 0.0) + jnp.where(ladder < limit, second, 0.0),
            axis=0,
            keepdims=True,
        )
    part_copies = [
        pltpu.make_async_remote_copy(
            src_ref=mine, dst_ref=parts.at[k - 1], send_sem=part_send.at[k - 1],
            recv_sem=part_recv.at[k - 1], device_id=peer(k), device_id_type=MESH,
        )
        for k in range(1, n_rad)
    ]
    for copy in part_copies:
        copy.start()
    for copy in part_copies:
        copy.wait_recv()
    pred = mine[...]
    for k in range(1, n_rad):
        pred = pred + parts[k - 1]
    res = jnp.where(live, (step_len * pred - observed) * inverse, 0.0)
    terms = res * inverse

    first = jnp.zeros((depth, pixels), f32)
    second = jnp.zeros((depth, pixels), f32)
    for m in range(slots):
        limit, term = local[m : m + 1, :], terms[m : m + 1, :]
        first = first + jnp.where(ladder <= limit, term, 0.0)
        second = second + jnp.where(ladder < limit, term, 0.0)
    first, second = first.T, second.T
    for q in range(8):
        suffix = (first, second)[q % 2][(q // 2) * cols : (q // 2 + 1) * cols]
        slopes[q, PAD : PAD + cols] = dens[q] * step_len * suffix

    def collect(u):
        sums = [None] * 3
        for v in range(3):
            for q in range(8):
                window = slopes[q, PAD + 1 - v : PAD + 1 - v + cols, :]
                for w in range(3):
                    term = weights[9 * u + 3 * v + w, q : q + 1, :] * window
                    sums[w] = term if sums[w] is None else sums[w] + term
        back_edges_out[0, u] = pack(sums[0][:, 0:1])
        back_edges_out[1, u] = pack(sums[2][:, depth - 1 : depth])
        low = jnp.where(lane == depth - 1, 0.0, pltpu.roll(sums[0], depth - 1, 1))
        high = jnp.where(lane == 0, 0.0, pltpu.roll(sums[2], 1, 1))
        return sums[1] + low + high

    own = None
    for u in (0, 2, 1):
        result = collect(u)
        if u == 1:
            own = result
        else:
            back_rows_out[u // 2] = result
        for n, (du, dz) in enumerate(AROUND):
            if du == u - 1:
                pl.when(exists(du, dz))(back_copies[n].start)

    grads = []
    for p in range(8):
        total = blocks[p]
        for q in range(8):
            total = total + mixing[q, p : p + 1, :] * slopes[q, PAD : PAD + cols, :]
        grads.append(total)
    even_lane = lane % 2 == 0
    for i in range(2):
        for j in range(2):
            q = 4 * i + 2 * j
            for side in range(2):
                index = side * half + lane // 2
                out_excite[side, i, pl.ds(j, cols, stride=2), :] = jnp.where(
                    even_lane, picked(grads[q], index), picked(grads[q + 1], index)
                )
    stores = [
        pltpu.make_async_copy(
            out_excite.at[side],
            grad_excite_hbm.at[:, :, pl.ds(side * depth, depth)],
            store_sem.at[side],
        )
        for side in range(2)
    ]
    for store in stores:
        store.start()

    for n, (du, dz) in enumerate(AROUND):
        pl.when(exists(-du, -dz))(back_copies[n].wait_recv)
    near = unpack(back_edges[0, 0] + back_edges[0, 1] + back_edges[0, 2])
    far = unpack(back_edges[1, 0] + back_edges[1, 1] + back_edges[1, 2])
    own = own + back_rows[0] + back_rows[1]
    own = own + jnp.where(lane == 0, near, 0.0) + jnp.where(lane == depth - 1, far, 0.0)
    out_coarse[...] = own
    stores.append(pltpu.make_async_copy(out_coarse, grad_coarse_hbm, store_sem.at[2]))
    stores[-1].start()
    for n, (du, dz) in enumerate(AROUND):
        pl.when(exists(du, dz))(halo_copies[n].wait_send)
        pl.when(exists(du, dz))(back_copies[n].wait_send)
    for copy in part_copies:
        copy.wait_send()
    for store in stores:
        store.wait()


def per_device(coarse, excite, kernels, mixing, star_bin, star_count, star_obs, star_isig):
    samples, rows, cols, depth = coarse.shape
    slots = star_bin.shape[2]
    n_ang, n_rad = lax.axis_size("ang"), lax.axis_size("rad")
    assert samples == 1 and rows == 1 and 4 * cols == depth
    f32 = jnp.float32
    vmem, dma = pltpu.VMEM, pltpu.SemaphoreType.DMA
    anywhere = pl.BlockSpec(memory_space=pl.ANY)
    padded = cols + 2 * PAD
    swap = lambda stars: jnp.swapaxes(stars, 1, 2)
    grad_excite, grad_coarse = pl.pallas_call(
        functools.partial(kernel, n_ang, n_rad),
        out_shape=[
            jax.ShapeDtypeStruct(excite.shape[1:], f32),
            jax.ShapeDtypeStruct((cols, depth), f32),
        ],
        in_specs=[anywhere] * 8,
        out_specs=[anywhere] * 2,
        scratch_shapes=[
            vmem((cols, depth), f32),
            vmem((2, 2, 2 * cols, depth), f32),
            vmem((27, 8, depth), f32),
            vmem((8, 8, depth), f32),
            vmem((2, slots, 2 * cols), jnp.int32),
            vmem((2, 2 * cols), jnp.int32),
            vmem((2, slots, 2 * cols), f32),
            vmem((2, slots, 2 * cols), f32),
            vmem((2, 1, depth), f32),
            vmem((2, cols, depth), f32),
            vmem((2, 3, 1, depth), f32),
            vmem((3, 3, padded, depth), f32),
            vmem((8, cols, depth), f32),
            vmem((8, cols, depth), f32),
            vmem((slots, depth), f32),
            vmem((n_rad - 1, slots, depth), f32),
            vmem((8, padded, depth), f32),
            vmem((2, cols, depth), f32),
            vmem((2, 3, 1, depth), f32),
            vmem((2, cols, depth), f32),
            vmem((2, 3, 1, depth), f32),
            vmem((2, 2, 2 * cols, depth), f32),
            vmem((cols, depth), f32),
            dma((9,)),
            dma((8,)),
            dma((8,)),
            dma((n_rad - 1,)),
            dma((n_rad - 1,)),
            dma((8,)),
            dma((8,)),
            dma((3,)),
        ],
        compiler_params=pltpu.CompilerParams(collective_id=0, has_side_effects=True),
    )(
        coarse[0, 0],
        excite[0],
        kernels,
        mixing,
        swap(star_bin),
        star_count,
        swap(star_obs),
        swap(star_isig),
    )
    return grad_excite[None], grad_coarse[None, None]


def solution(mesh):
    in_specs = (
        P(None, "ang", None, "rad"),
        P(None, "ang", None, "rad"),
        P(),
        P(),
        P("ang", None, None),
        P("ang", None),
        P("ang", None, None),
        P("ang", None, None),
    )
    out_specs = (P(None, "ang", None, "rad"), P(None, "ang", None, "rad"))
    return jax.shard_map(
        per_device, mesh=mesh, in_specs=in_specs, out_specs=out_specs, check_vma=False
    )
```

time: 215 us -> 18.5 us (0.09)
  local copies, waits for them, and re-layouts: 147 us -> 2.18 us
  starting transfers between devices: 24.6 us -> 0 us
  Pallas kernels: 0 us -> 15.5 us
  other arithmetic: 13.9 us -> 0 us
  blocking collectives: 13.4 us -> 0 us
  matrix products: 10.6 us -> 0 us
  waiting for transfers between devices: 3.03 us -> 0 us
    mul x59 -> x0, local copies, waits for them, and re-layouts: 43.4 us -> none  [the longest x57 35.3 us: per_device(): fine = fine + kernel_here[offset][:, None, None, None, :] * window[None]]
    reshape x4 -> x0, local copies, waits for them, and re-layouts: 35.7 us -> none  [the longest x1 10.5 us: to_blocks(): field.reshape(samples, na // 2, 2, nb // 2, 2, nr // 2, 2)]
    ppermute x8 -> x0, starting transfers between devices: 24.6 us -> none  [the longest x4 13.4 us: extended(): lax.ppermute(lax.slice_in_dim(block, block.shape[dim] - width, None, axis...]
    gather x3 -> x0, local copies, waits for them, and re-layouts: 20.7 us -> none  [per_device(): pred = jnp.take_along_axis(extinction, clipped[None], axis=3)]
    transpose x3 -> x0, local copies, waits for them, and re-layouts: 19 us -> none  [to_blocks(): return field.reshape(samples, na // 2, 2, nb // 2, 2, nr // 2, 2).transpo...]
    pallas_call x0 -> x1, Pallas kernels: none -> 15.5 us  [per_device(): pl.pallas_call(functools.partial(kernel, n_ang, n_rad), out_shape=[jax.Sh...]
    exp x2 -> x0, local copies, waits for them, and re-layouts: 14.9 us -> none  [per_device(): dens = jnp.exp(from_blocks(fine))]
    all_gather x2 -> x0, blocking collectives: 13.4 us -> none  [the longest x1 7.26 us: per_device(): every = lax.all_gather(depth_sums[None], 'rad', axis=0, tiled=True)]
  transfers between devices with their start and end apart: 8 -> 0, of which waited for: 1 -> 0; matrix products, arithmetic and copies ran while one was open for 34% -> 0% of each run, Pallas kernels for 0% -> 0%
where the time goes in v1:
time: 18.5 us; the launch traced here: 18.3 us
  Pallas kernels  15.5 us (84%)
  local copies, waits for them, and re-layouts  2.18 us (12%)
  between operations  0.65 us (4%)
    pallas_call x1, Pallas kernels, per_device(): pl.pallas_call(functools.partial(kernel, n_ang, n_rad), out_shape=[jax.Sh...  15.5 us
    unnamed x4, local copies, waits for them, and re-layouts  2.18 us

profile of v1, /device:TPU:1, one launch (start us, length us, event | category | flops | bytes accessed | tf_op | source)
XLA Modules:
  0.0 18.3 jit_solution(3280167467130183806)
XLA Ops:
  0.6 15.5 %shard_map.95 = (f32[2,64,256]{2,1,0:T(8,128)}, f32[32,128]{1,0:T(8,128)}) custom-call(f32[32,128]{1,0:T(8,128)} %bitcast.9, f32[2,64,256]{2,1,0:T(8,128)} %bitcast.8, f32[27,8,512]{2,1,0:T(8,128)} %weights_hbm.1, f32[8,8,512]{2,1,0:T(8,128)} %mixing_hbm.1, s32[2,16,64]{2,1,0:T(8,128)} %bitcast.10, s32[2,64]{1,0:T(2,128)} %count_hbm.1, ...), custom_call_target="tpu_custom_call" | custom-call | tf_op jit(solution)/shard_map/pallas_call | solution.py:358
  16.1 0.0 copy-start
  16.1 1.6 %copy.12 = f32[1,2,64,256]{3,2,1,0:T(8,128)} copy(f32[1,2,64,256]{3,2,1,0:T(8,128)} %bitcast.7) | data formatting | bytes 262144
  17.7 0.0 copy-done
  17.7 0.6 %copy.13 = f32[1,1,32,128]{3,2,1,0:T(8,128)} copy(f32[1,1,32,128]{3,2,1,0:T(8,128)S(1)} %bitcast.13) | data formatting | bytes 32768
Async XLA Ops:
  16.1 1.6 %copy-start = (f32[32,128]{1,0:T(8,128)S(1)}, f32[32,128]{1,0:T(8,128)}, u32[]{:S(2)}) copy-start(f32[32,128]{1,0:T(8,128)} %get-tuple-element.5) | copy-start | bytes 49156

commit v2 on v1

--- a/solution.py
+++ b/solution.py
@@ -23,8 +23,8 @@
     count_hbm,
     obs_hbm,
     isig_hbm,
-    grad_excite_hbm,
-    grad_coarse_hbm,
+    out_excite,
+    out_coarse,
     coarse,
     excite,
     weights,
@@ -46,8 +46,6 @@
     back_edges_out,
     back_rows,
     back_edges,
-    out_excite,
-    out_coarse,
     load_sem,
     halo_send,
     halo_recv,
@@ -55,7 +53,6 @@
     part_recv,
     back_send,
     back_recv,
-    store_sem,
 ):
     ang = lax.axis_index("ang")
     rad = lax.axis_index("rad")
@@ -153,12 +150,6 @@
     edge_out[0] = pack(middle[:, 0:1])
     edge_out[1] = pack(middle[:, depth - 1 : depth])
 
-    sides = [jnp.where(place > 0, 1, 0) + jnp.where(place < size - 1, 1, 0)
-             for place, size in ((ang, n_ang), (rad, n_rad))]
-    pl.semaphore_wait(barrier, sides[0] * (sides[1] + 1) + n_rad - 1)
-    for n, (du, dz) in enumerate(AROUND):
-        pl.when(exists(du, dz))(halo_copies[n].start)
-
     for load in loads[1:]:
         load.wait()
 
@@ -197,6 +188,12 @@
         for p in range(1, 8):
             total = total + mixing[q, p : p + 1, :] * children[p]
         fine.append(total)
+
+    sides = [jnp.where(place > 0, 1, 0) + jnp.where(place < size - 1, 1, 0)
+             for place, size in ((ang, n_ang), (rad, n_rad))]
+    pl.semaphore_wait(barrier, sides[0] * (sides[1] + 1) + n_rad - 1)
+    for n, (du, dz) in enumerate(AROUND):
+        pl.when(exists(du, dz))(halo_copies[n].start)
 
     blank = jnp.zeros((PAD, depth), f32)
     for u in range(3):
@@ -316,17 +313,6 @@
                 out_excite[side, i, pl.ds(j, cols, stride=2), :] = jnp.where(
                     even_lane, picked(grads[q], index), picked(grads[q + 1], index)
                 )
-    stores = [
-        pltpu.make_async_copy(
-            out_excite.at[side],
-            grad_excite_hbm.at[:, :, pl.ds(side * depth, depth)],
-            store_sem.at[side],
-        )
-        for side in range(2)
-    ]
-    for store in stores:
-        store.start()
-
     for n, (du, dz) in enumerate(AROUND):
         pl.when(exists(-du, -dz))(back_copies[n].wait_recv)
     near = unpack(back_edges[0, 0] + back_edges[0, 1] + back_edges[0, 2])
@@ -334,15 +320,25 @@
     own = own + back_rows[0] + back_rows[1]
     own = own + jnp.where(lane == 0, near, 0.0) + jnp.where(lane == depth - 1, far, 0.0)
     out_coarse[...] = own
-    stores.append(pltpu.make_async_copy(out_coarse, grad_coarse_hbm, store_sem.at[2]))
-    stores[-1].start()
     for n, (du, dz) in enumerate(AROUND):
         pl.when(exists(du, dz))(halo_copies[n].wait_send)
         pl.when(exists(du, dz))(back_copies[n].wait_send)
     for copy in part_copies:
         copy.wait_send()
-    for store in stores:
-        store.wait()
+
+
+def write(halves, block, grad_excite, grad_coarse, sem):
+    depth = block.shape[1]
+    pairs = [(halves.at[side], grad_excite.at[:, :, pl.ds(side * depth, depth)]) for side in range(2)]
+    pairs.append((block, grad_coarse))
+    copies = [
+        pltpu.make_async_copy(source, target, sem.at[n])
+        for n, (source, target) in enumerate(pairs)
+    ]
+    for copy in copies:
+        copy.start()
+    for copy in copies:
+        copy.wait()
 
 
 def per_device(coarse, excite, kernels, mixing, star_bin, star_count, star_obs, star_isig):
@@ -355,14 +351,11 @@
     anywhere = pl.BlockSpec(memory_space=pl.ANY)
     padded = cols + 2 * PAD
     swap = lambda stars: jnp.swapaxes(stars, 1, 2)
-    grad_excite, grad_coarse = pl.pallas_call(
+    results = pl.pallas_call(
         functools.partial(kernel, n_ang, n_rad),
-        out_shape=[
-            jax.ShapeDtypeStruct(excite.shape[1:], f32),
-            jax.ShapeDtypeStruct((cols, depth), f32),
-        ],
-        in_specs=[anywhere] * 8,
-        out_specs=[anywhere] * 2,
+        out_shape=[vmem((2, 2, 2 * cols, depth), f32), vmem((cols, depth), f32)],
+        in_specs=[pl.BlockSpec(memory_space=pltpu.HBM)] * 8,
+        out_specs=[pl.BlockSpec(memory_space=vmem)] * 2,
         scratch_shapes=[
             vmem((cols, depth), f32),
             vmem((2, 2, 2 * cols, depth), f32),
@@ -385,8 +378,6 @@
             vmem((2, 3, 1, depth), f32),
             vmem((2, cols, depth), f32),
             vmem((2, 3, 1, depth), f32),
-            vmem((2, 2, 2 * cols, depth), f32),
-            vmem((cols, depth), f32),
             dma((9,)),
             dma((8,)),
             dma((8,)),
@@ -394,19 +385,36 @@
             dma((n_rad - 1,)),
             dma((8,)),
             dma((8,)),
-            dma((3,)),
         ],
-        compiler_params=pltpu.CompilerParams(collective_id=0, has_side_effects=True),
+        compiler_params=pltpu.CompilerParams(
+            collective_id=0, has_side_effects=True, vmem_limit_bytes=8 << 20
+        ),
     )(
-        coarse[0, 0],
-        excite[0],
-        kernels,
-        mixing,
-        swap(star_bin),
-        star_count,
-        swap(star_obs),
-        swap(star_isig),
+        *(
+            pltpu.with_memory_space_constraint(argument, pltpu.HBM)
+            for argument in (
+                coarse[0, 0],
+                excite[0],
+                kernels,
+                mixing,
+                swap(star_bin),
+                star_count,
+                swap(star_obs),
+                swap(star_isig),
+            )
+        )
     )
+    grad_excite, grad_coarse = pl.pallas_call(
+        write,
+        out_shape=[
+            jax.ShapeDtypeStruct(excite.shape[1:], f32),
+            jax.ShapeDtypeStruct((cols, depth), f32),
+        ],
+        in_specs=[anywhere] * 2,
+        out_specs=[pl.BlockSpec(memory_space=pltpu.HBM)] * 2,
+        scratch_shapes=[dma((3,))],
+        compiler_params=pltpu.CompilerParams(vmem_limit_bytes=1 << 20),
+    )(*results)
     return grad_excite[None], grad_coarse[None, None]
 
 

time: 18.5 us -> 16.4 us (0.89)
  local copies, waits for them, and re-layouts: 2.18 us -> 0 us
    unnamed x4 -> x0, local copies, waits for them, and re-layouts: 2.18 us -> none
    pallas_call x1 -> x2, Pallas kernels: 15.5 us -> 15.5 us  [the longest x1 14.9 us: per_device(): pl.pallas_call(functools.partial(kernel, n_ang, n_rad), out_shape=[vmem((...]
where the time goes in v2:
time: 16.4 us; the launch traced here: 16.2 us
  Pallas kernels  15.5 us (95%)
  between operations  0.64 us (4%)
    pallas_call x1, Pallas kernels, per_device(): pl.pallas_call(functools.partial(kernel, n_ang, n_rad), out_shape=[vmem((...  14.9 us
    pallas_call x1, Pallas kernels, per_device(): pl.pallas_call(write, out_shape=[jax.ShapeDtypeStruct(excite.shape[1:], f...  0.68 us

profile of v2, /device:TPU:1, one launch (start us, length us, event | category | flops | bytes accessed | tf_op | source)
XLA Modules:
  0.0 16.2 jit_solution(7187954247381915824)
XLA Ops:
  0.6 14.9 %shard_map.95 = (f32[2,2,64,128]{3,2,1,0:T(8,128)S(1)}, f32[32,128]{1,0:T(8,128)S(1)}) custom-call(f32[32,128]{1,0:T(8,128)} %bitcast.8, f32[2,64,256]{2,1,0:T(8,128)} %bitcast.7, f32[27,8,512]{2,1,0:T(8,128)} %weights_hbm.1, f32[8,8,512]{2,1,0:T(8,128)} %mixing_hbm.1, s32[2,16,64]{2,1,0:T(8,128)} %bitcast.9, s32[2,64]{1,0:T(2,128)} %count_hbm.1, ...), custom_call_target="tpu_custom_call" | custom-call | tf_op jit(solution)/shard_map/pallas_call | solution.py:354
  15.5 0.7 %shard_map.96 = (f32[2,64,256]{2,1,0:T(8,128)}, f32[32,128]{1,0:T(8,128)}) custom-call(f32[2,2,64,128]{3,2,1,0:T(8,128)S(1)} %get-tuple-element.6.halves, f32[32,128]{1,0:T(8,128)S(1)} %get-tuple-element.7.block), custom_call_target="tpu_custom_call" | custom-call | tf_op jit(solution)/shard_map/pallas_call | solution.py:407

commit v3 on v2

--- a/solution.py
+++ b/solution.py
@@ -9,6 +9,7 @@
 
 MESH = pl.DeviceIdType.MESH
 AROUND = [(du, dz) for du in (-1, 0, 1) for dz in (-1, 0, 1) if (du, dz) != (0, 0)]
+AROUND.sort(key=lambda step: -abs(step[0]) - abs(step[1]))
 PAD = 8
 
 
@@ -93,8 +94,7 @@
         pltpu.make_async_copy(source, target, load_sem.at[n])
         for n, (source, target) in enumerate(pairs)
     ]
-    for load in loads:
-        load.start()
+    loads[0].start()
 
     barrier = pltpu.get_barrier_semaphore()
     beside = [(du, dz) for du, dz in AROUND if du != 0]
@@ -106,9 +106,11 @@
 
     for k in range(1, n_rad):
         pl.semaphore_signal(barrier, inc=1, device_id=peer(k), device_id_type=MESH)
+    for load in loads[1:]:
+        load.start()
 
     rows_of = lambda du: 0 if du < 0 else 1
-    halo_copies, back_copies = [], []
+    halo_copies, back_copies, targets = [], [], []
     for n, (du, dz) in enumerate(AROUND):
         if dz == 0:
             source, target = coarse, halo_rows.at[rows_of(-du)]
@@ -129,26 +131,35 @@
                 recv_sem=back_recv.at[n], device_id=at(du, dz), device_id_type=MESH,
             )
         )
+        targets.append((target, back_target))
+
+    lane = lax.broadcasted_iota(jnp.int32, (cols, depth), 1)
+    row = lax.broadcasted_iota(jnp.int32, (cols, depth), 0)
+    diagonal = lane == row
+
+    def pack(column):
+        return jnp.sum(jnp.where(diagonal, column, 0.0), axis=0, keepdims=True)
+
+    def unpack(packed):
+        return jnp.sum(jnp.where(diagonal, packed, 0.0), axis=1, keepdims=True)
+
+    loads[0].wait()
+    middle = coarse[...]
+    edge_out[0] = pack(middle[:, 0:1])
+    edge_out[1] = pack(middle[:, depth - 1 : depth])
+
+    sides = [jnp.where(place > 0, 1, 0) + jnp.where(place < size - 1, 1, 0)
+             for place, size in ((ang, n_ang), (rad, n_rad))]
+    pl.semaphore_wait(barrier, sides[0] * (sides[1] + 1) + n_rad - 1)
+    for n, (du, dz) in enumerate(AROUND):
+        pl.when(exists(du, dz))(halo_copies[n].start)
+
+    for (du, dz), (target, back_target) in zip(AROUND, targets):
 
         @pl.when(jnp.logical_not(exists(-du, -dz)))
         def _():
             target[...] = jnp.zeros(target.shape, f32)
             back_target[...] = jnp.zeros(back_target.shape, f32)
-
-    lane = lax.broadcasted_iota(jnp.int32, (cols, depth), 1)
-    row = lax.broadcasted_iota(jnp.int32, (cols, depth), 0)
-    diagonal = lane == row
-
-    def pack(column):
-        return jnp.sum(jnp.where(diagonal, column, 0.0), axis=0, keepdims=True)
-
-    def unpack(packed):
-        return jnp.sum(jnp.where(diagonal, packed, 0.0), axis=1, keepdims=True)
-
-    loads[0].wait()
-    middle = coarse[...]
-    edge_out[0] = pack(middle[:, 0:1])
-    edge_out[1] = pack(middle[:, depth - 1 : depth])
 
     for load in loads[1:]:
         load.wait()
@@ -189,12 +200,6 @@
             total = total + mixing[q, p : p + 1, :] * children[p]
         fine.append(total)
 
-    sides = [jnp.where(place > 0, 1, 0) + jnp.where(place < size - 1, 1, 0)
-             for place, size in ((ang, n_ang), (rad, n_rad))]
-    pl.semaphore_wait(barrier, sides[0] * (sides[1] + 1) + n_rad - 1)
-    for n, (du, dz) in enumerate(AROUND):
-        pl.when(exists(du, dz))(halo_copies[n].start)
-
     blank = jnp.zeros((PAD, depth), f32)
     for u in range(3):
         for w in range(3):
@@ -208,7 +213,6 @@
         near, far = unpack(halo_edges[0, u]), unpack(halo_edges[1, u])
         inner = pl.ds(PAD, cols)
         windows[u, 0, inner] = jnp.where(lane == 0, near, pltpu.roll(base, 1, 1))
-        windows[u, 1, inner] = base
         windows[u, 2, inner] = jnp.where(lane == depth - 1, far, pltpu.roll(base, depth - 1, 1))
 
     def spread(u, ws, fine):
@@ -223,14 +227,22 @@
 
     windows[1, 1, PAD : PAD + cols] = middle
     fine = spread(1, (1,), fine)
-    for n, (du, dz) in enumerate(AROUND):
-        pl.when(exists(-du, -dz))(halo_copies[n].wait_recv)
+    def arrived(choose):
+        for n, (du, dz) in enumerate(AROUND):
+            if choose(du, dz):
+                pl.when(exists(-du, -dz))(halo_copies[n].wait_recv)
+
+    arrived(lambda du, dz: du == 0)
     gather(1, middle)
-    gather(0, halo_rows[0])
-    gather(2, halo_rows[1])
     fine = spread(1, (0, 2), fine)
-    fine = spread(0, (0, 1, 2), fine)
-    fine = spread(2, (0, 1, 2), fine)
+    arrived(lambda du, dz: dz == 0)
+    for u in (0, 2):
+        windows[u, 1, PAD : PAD + cols] = halo_rows[u // 2]
+        fine = spread(u, (1,), fine)
+    arrived(lambda du, dz: du != 0 and dz != 0)
+    for u in (0, 2):
+        gather(u, halo_rows[u // 2])
+        fine = spread(u, (0, 2), fine)
     for q in range(8):
         dens[q] = jnp.exp(fine[q])
 

time: 16.4 us -> 16.4 us (level)
  no operation moved by 1% of the time
where the time goes in v3:
time: 16.4 us; the launch traced here: 16.1 us
  Pallas kernels  15.5 us (95%)
  between operations  0.64 us (4%)
    pallas_call x1, Pallas kernels, per_device(): pl.pallas_call(functools.partial(kernel, n_ang, n_rad), out_shape=[vmem((...  14.8 us
    pallas_call x1, Pallas kernels, per_device(): pl.pallas_call(write, out_shape=[jax.ShapeDtypeStruct(excite.shape[1:], f...  0.68 us

profile of v3, /device:TPU:1, one launch (start us, length us, event | category | flops | bytes accessed | tf_op | source)
XLA Modules:
  0.0 16.1 jit_solution(7009080167293046943)
XLA Ops:
  0.6 14.8 %shard_map.95 = (f32[2,2,64,128]{3,2,1,0:T(8,128)S(1)}, f32[32,128]{1,0:T(8,128)S(1)}) custom-call(f32[32,128]{1,0:T(8,128)} %bitcast.8, f32[2,64,256]{2,1,0:T(8,128)} %bitcast.7, f32[27,8,512]{2,1,0:T(8,128)} %weights_hbm.1, f32[8,8,512]{2,1,0:T(8,128)} %mixing_hbm.1, s32[2,16,64]{2,1,0:T(8,128)} %bitcast.9, s32[2,64]{1,0:T(2,128)} %count_hbm.1, ...), custom_call_target="tpu_custom_call" | custom-call | tf_op jit(solution)/shard_map/pallas_call | solution.py:366
  15.4 0.7 %shard_map.96 = (f32[2,64,256]{2,1,0:T(8,128)}, f32[32,128]{1,0:T(8,128)}) custom-call(f32[2,2,64,128]{3,2,1,0:T(8,128)S(1)} %get-tuple-element.6.halves, f32[32,128]{1,0:T(8,128)S(1)} %get-tuple-element.7.block), custom_call_target="tpu_custom_call" | custom-call | tf_op jit(solution)/shard_map/pallas_call | solution.py:419

commit v4 on v3

--- a/solution.py
+++ b/solution.py
@@ -11,6 +11,7 @@
 AROUND = [(du, dz) for du in (-1, 0, 1) for dz in (-1, 0, 1) if (du, dz) != (0, 0)]
 AROUND.sort(key=lambda step: -abs(step[0]) - abs(step[1]))
 PAD = 8
+UNROLL = 4
 
 
 def kernel(
@@ -42,6 +43,8 @@
     dens,
     mine,
     parts,
+    local,
+    terms,
     slopes,
     back_rows_out,
     back_edges_out,
@@ -179,26 +182,26 @@
     inverse = picked(jnp.where(slot < counts, wide(isig), 0.0), order)
     live = inverse > 0.0
     observed = picked(wide(obs), order)
-    local = picked(wide(bins), order) - rad * (2 * depth)
+    local[...] = picked(wide(bins), order) - rad * (2 * depth)
 
     evens = (2 * lane) % depth + lane // half
     odds = (2 * lane + 1) % depth - lane // half
-    children = [None] * 8
-    for i in range(2):
+
+    def split(i, carry):
         for j in range(2):
             low = picked(excite[0, i, pl.ds(j, cols, stride=2), :], evens)
             high = picked(excite[1, i, pl.ds(j, cols, stride=2), :], odds)
-            q = 4 * i + 2 * j
-            children[q] = jnp.where(lane < half, low, high)
-            children[q + 1] = pltpu.roll(jnp.where(lane < half, high, low), half, 1)
-            blocks[q] = children[q]
-            blocks[q + 1] = children[q + 1]
-    fine = []
-    for q in range(8):
-        total = mixing[q, 0:1, :] * children[0]
-        for p in range(1, 8):
-            total = total + mixing[q, p : p + 1, :] * children[p]
-        fine.append(total)
+            blocks[4 * i + 2 * j] = jnp.where(lane < half, low, high)
+            blocks[4 * i + 2 * j + 1] = pltpu.roll(jnp.where(lane < half, high, low), half, 1)
+        return carry
+
+    lax.fori_loop(0, 2, split, 0)
+
+    def mix(p, fine):
+        child = blocks[p]
+        return tuple(fine[q] + mixing[q, pl.ds(p, 1), :] * child for q in range(8))
+
+    fine = lax.fori_loop(0, 8, mix, tuple(jnp.zeros((cols, depth), f32) for _ in range(8)))
 
     blank = jnp.zeros((PAD, depth), f32)
     for u in range(3):
@@ -213,36 +216,23 @@
         near, far = unpack(halo_edges[0, u]), unpack(halo_edges[1, u])
         inner = pl.ds(PAD, cols)
         windows[u, 0, inner] = jnp.where(lane == 0, near, pltpu.roll(base, 1, 1))
+        windows[u, 1, inner] = base
         windows[u, 2, inner] = jnp.where(lane == depth - 1, far, pltpu.roll(base, depth - 1, 1))
 
-    def spread(u, ws, fine):
+    def spread(u, fine):
         for v in range(3):
-            for w in ws:
+            for w in range(3):
                 window = windows[u, w, PAD - 1 + v : PAD - 1 + v + cols, :]
                 t = 9 * u + 3 * v + w
-                fine = [
-                    fine[q] + weights[t, q : q + 1, :] * window for q in range(8)
-                ]
+                fine = tuple(fine[q] + weights[t, q : q + 1, :] * window for q in range(8))
         return fine
 
-    windows[1, 1, PAD : PAD + cols] = middle
-    fine = spread(1, (1,), fine)
-    def arrived(choose):
-        for n, (du, dz) in enumerate(AROUND):
-            if choose(du, dz):
-                pl.when(exists(-du, -dz))(halo_copies[n].wait_recv)
-
-    arrived(lambda du, dz: du == 0)
+    for n, (du, dz) in enumerate(AROUND):
+        pl.when(exists(-du, -dz))(halo_copies[n].wait_recv)
+    gather(0, halo_rows[0])
     gather(1, middle)
-    fine = spread(1, (0, 2), fine)
-    arrived(lambda du, dz: dz == 0)
-    for u in (0, 2):
-        windows[u, 1, PAD : PAD + cols] = halo_rows[u // 2]
-        fine = spread(u, (1,), fine)
-    arrived(lambda du, dz: du != 0 and dz != 0)
-    for u in (0, 2):
-        gather(u, halo_rows[u // 2])
-        fine = spread(u, (0, 2), fine)
+    gather(2, halo_rows[1])
+    fine = lax.fori_loop(0, 3, spread, fine)
     for q in range(8):
         dens[q] = jnp.exp(fine[q])
 
@@ -250,13 +240,19 @@
     ladder = 2 * lax.broadcasted_iota(jnp.int32, (depth, pixels), 0)
     first = jnp.concatenate([dens[q] for q in range(0, 8, 2)], axis=0).T
     second = jnp.concatenate([dens[q] for q in range(1, 8, 2)], axis=0).T
-    for m in range(slots):
-        limit = local[m : m + 1, :]
-        mine[m : m + 1, :] = jnp.sum(
-            jnp.where(ladder <= limit, first, 0.0) + jnp.where(ladder < limit, second, 0.0),
-            axis=0,
-            keepdims=True,
-        )
+
+    def reach(step, carry):
+        for n in range(UNROLL):
+            m = pl.ds(step * UNROLL + n, 1)
+            limit = local[m, :]
+            mine[m, :] = jnp.sum(
+                jnp.where(ladder <= limit, first, 0.0) + jnp.where(ladder < limit, second, 0.0),
+                axis=0,
+                keepdims=True,
+            )
+        return carry
+
+    lax.fori_loop(0, slots // UNROLL, reach, 0)
     part_copies = [
         pltpu.make_async_remote_copy(
             src_ref=mine, dst_ref=parts.at[k - 1], send_sem=part_send.at[k - 1],
@@ -272,27 +268,34 @@
     for k in range(1, n_rad):
         pred = pred + parts[k - 1]
     res = jnp.where(live, (step_len * pred - observed) * inverse, 0.0)
-    terms = res * inverse
-
-    first = jnp.zeros((depth, pixels), f32)
-    second = jnp.zeros((depth, pixels), f32)
-    for m in range(slots):
-        limit, term = local[m : m + 1, :], terms[m : m + 1, :]
-        first = first + jnp.where(ladder <= limit, term, 0.0)
-        second = second + jnp.where(ladder < limit, term, 0.0)
+    terms[...] = res * inverse
+
+    def collected(step, sums):
+        first, second = sums
+        for n in range(UNROLL):
+            m = pl.ds(step * UNROLL + n, 1)
+            limit, term = local[m, :], terms[m, :]
+            first = first + jnp.where(ladder <= limit, term, 0.0)
+            second = second + jnp.where(ladder < limit, term, 0.0)
+        return first, second
+
+    nothing = jnp.zeros((depth, pixels), f32)
+    first, second = lax.fori_loop(0, slots // UNROLL, collected, (nothing, nothing))
     first, second = first.T, second.T
     for q in range(8):
         suffix = (first, second)[q % 2][(q // 2) * cols : (q // 2 + 1) * cols]
         slopes[q, PAD : PAD + cols] = dens[q] * step_len * suffix
 
     def collect(u):
-        sums = [None] * 3
-        for v in range(3):
-            for q in range(8):
+        def child(q, sums):
+            sums = list(sums)
+            for v in range(3):
                 window = slopes[q, PAD + 1 - v : PAD + 1 - v + cols, :]
                 for w in range(3):
-                    term = weights[9 * u + 3 * v + w, q : q + 1, :] * window
-                    sums[w] = term if sums[w] is None else sums[w] + term
+                    sums[w] = sums[w] + weights[9 * u + 3 * v + w, pl.ds(q, 1), :] * window
+            return tuple(sums)
+
+        sums = lax.fori_loop(0, 8, child, tuple(jnp.zeros((cols, depth), f32) for _ in range(3)))
         back_edges_out[0, u] = pack(sums[0][:, 0:1])
         back_edges_out[1, u] = pack(sums[2][:, depth - 1 : depth])
         low = jnp.where(lane == depth - 1, 0.0, pltpu.roll(sums[0], depth - 1, 1))
@@ -310,21 +313,27 @@
             if du == u - 1:
                 pl.when(exists(du, dz))(back_copies[n].start)
 
-    grads = []
+    def unmix(q, grads):
+        slope = slopes[q, PAD : PAD + cols, :]
+        return tuple(grads[p] + mixing[q, p : p + 1, :] * slope for p in range(8))
+
+    grads = lax.fori_loop(0, 8, unmix, tuple(blocks[p] for p in range(8)))
     for p in range(8):
-        total = blocks[p]
-        for q in range(8):
-            total = total + mixing[q, p : p + 1, :] * slopes[q, PAD : PAD + cols, :]
-        grads.append(total)
+        dens[p] = grads[p]
     even_lane = lane % 2 == 0
-    for i in range(2):
+
+    def join(i, carry):
         for j in range(2):
-            q = 4 * i + 2 * j
+            even, odd = dens[4 * i + 2 * j], dens[4 * i + 2 * j + 1]
             for side in range(2):
                 index = side * half + lane // 2
                 out_excite[side, i, pl.ds(j, cols, stride=2), :] = jnp.where(
-                    even_lane, picked(grads[q], index), picked(grads[q + 1], index)
+                    even_lane, picked(even, index), picked(odd, index)
                 )
+        return carry
+
+    lax.fori_loop(0, 2, join, 0)
+
     for n, (du, dz) in enumerate(AROUND):
         pl.when(exists(-du, -dz))(back_copies[n].wait_recv)
     near = unpack(back_edges[0, 0] + back_edges[0, 1] + back_edges[0, 2])
@@ -357,7 +366,7 @@
     samples, rows, cols, depth = coarse.shape
     slots = star_bin.shape[2]
     n_ang, n_rad = lax.axis_size("ang"), lax.axis_size("rad")
-    assert samples == 1 and rows == 1 and 4 * cols == depth
+    assert slots % UNROLL == 0 and samples == 1 and rows == 1 and 4 * cols == depth
     f32 = jnp.float32
     vmem, dma = pltpu.VMEM, pltpu.SemaphoreType.DMA
     anywhere = pl.BlockSpec(memory_space=pl.ANY)
@@ -385,6 +394,8 @@
             vmem((8, cols, depth), f32),
             vmem((slots, depth), f32),
             vmem((n_rad - 1, slots, depth), f32),
+            vmem((slots, depth), jnp.int32),
+            vmem((slots, depth), f32),
             vmem((8, padded, depth), f32),
             vmem((2, cols, depth), f32),
             vmem((2, 3, 1, depth), f32),

time: 16.4 us -> 16.8 us (1.024)
  Pallas kernels: 15.5 us -> 15.9 us
    pallas_call x1, Pallas kernels: 14.8 us -> 15.2 us  [per_device(): pl.pallas_call(functools.partial(kernel, n_ang, n_rad), out_shape=[vmem((...]
where the time goes in v4:
time: 16.8 us; the launch traced here: 16.5 us
  Pallas kernels  15.9 us (95%)
  between operations  0.64 us (4%)
    pallas_call x1, Pallas kernels, per_device(): pl.pallas_call(functools.partial(kernel, n_ang, n_rad), out_shape=[vmem((...  15.2 us
    pallas_call x1, Pallas kernels, per_device(): pl.pallas_call(write, out_shape=[jax.ShapeDtypeStruct(excite.shape[1:], f...  0.68 us

profile of v4, /device:TPU:1, one launch (start us, length us, event | category | flops | bytes accessed | tf_op | source)
XLA Modules:
  0.0 16.5 jit_solution(13636553319896993682)
XLA Ops:
  0.6 15.2 %shard_map.95 = (f32[2,2,64,128]{3,2,1,0:T(8,128)S(1)}, f32[32,128]{1,0:T(8,128)S(1)}) custom-call(f32[32,128]{1,0:T(8,128)} %bitcast.8, f32[2,64,256]{2,1,0:T(8,128)} %bitcast.7, f32[27,8,512]{2,1,0:T(8,128)} %weights_hbm.1, f32[8,8,512]{2,1,0:T(8,128)} %mixing_hbm.1, s32[2,16,64]{2,1,0:T(8,128)} %bitcast.9, s32[2,64]{1,0:T(2,128)} %count_hbm.1, ...), custom_call_target="tpu_custom_call" | custom-call | tf_op jit(solution)/shard_map/pallas_call | solution.py:375
  15.9 0.7 %shard_map.96 = (f32[2,64,256]{2,1,0:T(8,128)}, f32[32,128]{1,0:T(8,128)}) custom-call(f32[2,2,64,128]{3,2,1,0:T(8,128)S(1)} %get-tuple-element.6.halves, f32[32,128]{1,0:T(8,128)S(1)} %get-tuple-element.7.block), custom_call_target="tpu_custom_call" | custom-call | tf_op jit(solution)/shard_map/pallas_call | solution.py:430

commit v5 on v3

--- a/solution.py
+++ b/solution.py
@@ -11,6 +11,7 @@
 AROUND = [(du, dz) for du in (-1, 0, 1) for dz in (-1, 0, 1) if (du, dz) != (0, 0)]
 AROUND.sort(key=lambda step: -abs(step[0]) - abs(step[1]))
 PAD = 8
+SHARES = 2
 
 
 def kernel(
@@ -250,40 +251,48 @@
     ladder = 2 * lax.broadcasted_iota(jnp.int32, (depth, pixels), 0)
     first = jnp.concatenate([dens[q] for q in range(0, 8, 2)], axis=0).T
     second = jnp.concatenate([dens[q] for q in range(1, 8, 2)], axis=0).T
-    for m in range(slots):
-        limit = local[m : m + 1, :]
-        mine[m : m + 1, :] = jnp.sum(
-            jnp.where(ladder <= limit, first, 0.0) + jnp.where(ladder < limit, second, 0.0),
-            axis=0,
-            keepdims=True,
-        )
-    part_copies = [
-        pltpu.make_async_remote_copy(
-            src_ref=mine, dst_ref=parts.at[k - 1], send_sem=part_send.at[k - 1],
-            recv_sem=part_recv.at[k - 1], device_id=peer(k), device_id_type=MESH,
-        )
-        for k in range(1, n_rad)
-    ]
-    for copy in part_copies:
-        copy.start()
-    for copy in part_copies:
-        copy.wait_recv()
-    pred = mine[...]
-    for k in range(1, n_rad):
-        pred = pred + parts[k - 1]
-    res = jnp.where(live, (step_len * pred - observed) * inverse, 0.0)
-    terms = res * inverse
+    share = slots // SHARES
+    part_copies = []
+    for group in range(SHARES):
+        for m in range(group * share, (group + 1) * share):
+            limit = local[m : m + 1, :]
+            mine[m : m + 1, :] = jnp.sum(
+                jnp.where(ladder <= limit, first, 0.0) + jnp.where(ladder < limit, second, 0.0),
+                axis=0,
+                keepdims=True,
+            )
+        slab = pl.ds(group * share, share)
+        for k in range(1, n_rad):
+            part_copies.append(
+                pltpu.make_async_remote_copy(
+                    src_ref=mine.at[slab], dst_ref=parts.at[k - 1, slab],
+                    send_sem=part_send.at[group, k - 1], recv_sem=part_recv.at[group, k - 1],
+                    device_id=peer(k), device_id_type=MESH,
+                )
+            )
+            part_copies[-1].start()
 
     first = jnp.zeros((depth, pixels), f32)
     second = jnp.zeros((depth, pixels), f32)
-    for m in range(slots):
-        limit, term = local[m : m + 1, :], terms[m : m + 1, :]
-        first = first + jnp.where(ladder <= limit, term, 0.0)
-        second = second + jnp.where(ladder < limit, term, 0.0)
+    for group in range(SHARES):
+        slab = slice(group * share, (group + 1) * share)
+        for copy in part_copies[group * (n_rad - 1) : (group + 1) * (n_rad - 1)]:
+            copy.wait_recv()
+        pred = mine[slab]
+        for k in range(1, n_rad):
+            pred = pred + parts[k - 1, slab]
+        weight = inverse[slab]
+        res = jnp.where(live[slab], (step_len * pred - observed[slab]) * weight, 0.0)
+        terms = res * weight * step_len
+        for m in range(share):
+            limit = local[group * share + m : group * share + m + 1, :]
+            term = terms[m : m + 1, :]
+            first = first + jnp.where(ladder <= limit, term, 0.0)
+            second = second + jnp.where(ladder < limit, term, 0.0)
     first, second = first.T, second.T
     for q in range(8):
         suffix = (first, second)[q % 2][(q // 2) * cols : (q // 2 + 1) * cols]
-        slopes[q, PAD : PAD + cols] = dens[q] * step_len * suffix
+        slopes[q, PAD : PAD + cols] = dens[q] * suffix
 
     def collect(u):
         sums = [None] * 3
@@ -393,8 +402,8 @@
             dma((9,)),
             dma((8,)),
             dma((8,)),
-            dma((n_rad - 1,)),
-            dma((n_rad - 1,)),
+            dma((SHARES, n_rad - 1)),
+            dma((SHARES, n_rad - 1)),
             dma((8,)),
             dma((8,)),
         ],

time: 16.4 us -> 16.4 us (level)
  no operation moved by 1% of the time
where the time goes in v5:
time: 16.4 us; the launch traced here: 16.2 us
  Pallas kernels  15.5 us (95%)
  between operations  0.64 us (4%)
    pallas_call x1, Pallas kernels, per_device(): pl.pallas_call(functools.partial(kernel, n_ang, n_rad), out_shape=[vmem((...  14.8 us
    pallas_call x1, Pallas kernels, per_device(): pl.pallas_call(write, out_shape=[jax.ShapeDtypeStruct(excite.shape[1:], f...  0.68 us

profile of v5, /device:TPU:1, one launch (start us, length us, event | category | flops | bytes accessed | tf_op | source)
XLA Modules:
  0.0 16.2 jit_solution(17324805690204772320)
XLA Ops:
  0.6 14.8 %shard_map.95 = (f32[2,2,64,128]{3,2,1,0:T(8,128)S(1)}, f32[32,128]{1,0:T(8,128)S(1)}) custom-call(f32[32,128]{1,0:T(8,128)} %bitcast.8, f32[2,64,256]{2,1,0:T(8,128)} %bitcast.7, f32[27,8,512]{2,1,0:T(8,128)} %weights_hbm.1, f32[8,8,512]{2,1,0:T(8,128)} %mixing_hbm.1, s32[2,16,64]{2,1,0:T(8,128)} %bitcast.9, s32[2,64]{1,0:T(2,128)} %count_hbm.1, ...), custom_call_target="tpu_custom_call" | custom-call | tf_op jit(solution)/shard_map/pallas_call | solution.py:375
  15.5 0.7 %shard_map.96 = (f32[2,64,256]{2,1,0:T(8,128)}, f32[32,128]{1,0:T(8,128)}) custom-call(f32[2,2,64,128]{3,2,1,0:T(8,128)S(1)} %get-tuple-element.6.halves, f32[32,128]{1,0:T(8,128)S(1)} %get-tuple-element.7.block), custom_call_target="tpu_custom_call" | custom-call | tf_op jit(solution)/shard_map/pallas_call | solution.py:428
